TPU v7x, 32 devices: a whole 2x2x4 slice. The times are simulated.
32 devices in a mesh: grp: 2 (over x), ep: 16 (over z, y, core).
Axes of the slice: x: 2, y: 2, z: 4, core: 2. Of those that a mesh axis runs over, the one named last changes fastest.
Arguments:
- states: bfloat16 [2, 1280, 2048], P(None, ('grp', 'ep')), may hold values from -6 to 6
- route_ids: int32 [2, 1280, 8], P(None, ('grp', 'ep')), may hold values from 0 to 15, all different within a row; in each aligned block of 40 rows (0 to 39, 40 to 79, ..., all dimensions but the last counted through in order) at most 30 rows name the same one
- route_gates: float32 [2, 1280, 8], P(None, ('grp', 'ep')), may hold values from 0.02 to 0.3
- moe_gain: float32 [2048], replicated, may hold values from 0.25 to 1.75
- final_gain: float32 [2048], replicated, may hold values from 0.25 to 1.75
- gate_proj: bfloat16 [16, 2048, 512], P('ep', 'grp'), may hold values from -0.125 to 0.125
- up_proj: bfloat16 [16, 2048, 512], P('ep', 'grp'), may hold values from -0.125 to 0.125
- down_proj: bfloat16 [16, 512, 2048], P('ep', 'grp'), may hold values from -0.25 to 0.25
- old_slots: int32 [16], replicated, may hold values from 0 to 15, each once
- new_slots: int32 [16], replicated, may hold values from 0 to 15, each once
- req_lengths: int32 [2, 2, 4], P(None, 'grp'), may hold values from 1 to 320, 640 in all within a row
- head_proj: bfloat16 [2048, 49152], P(None, ('grp', 'ep')), may hold values from -14 to 14
Outputs:
- mixed: bfloat16 [2, 1280, 2048], P(None, ('grp', 'ep'))
- moved_gate: bfloat16 [16, 2048, 512], P('ep', 'grp')
- moved_up: bfloat16 [16, 2048, 512], P('ep', 'grp')
- moved_down: bfloat16 [16, 512, 2048], P('ep', 'grp')
- log_probs: float32 [2, 8, 49152], P(None, None, ('grp', 'ep'))
Inputs may be any that keep to these rules, and one draw needn't show every extreme that they name: `route_ids`: in each aligned block of 40 rows (the rows of one device in one batch) no expert is named by more than 30 rows, a bound that some block reaches; the 8 ids of a row differ. `old_slots`: each expert once. `new_slots`: each expert once. `req_lengths`: the 4 lengths of a group in a batch sum to 640, and the largest is 320.
All inputs are finite; a program needn't handle non-finite values.
Results may differ from a plain program's by a relative error of at most 0.0035.
Values may be sent and summed in bfloat16 or wider, within the bound.
A program may use at most 128 MiB of HBM per device.

v0:
```python
import jax
import jax.numpy as jnp
from jax import lax
from jax.sharding import PartitionSpec as P


def normalize(rows, gain):
    scale = lax.rsqrt(jnp.mean(rows * rows, axis=-1, keepdims=True) + 1e-06)
    return (rows * scale * gain).astype(jnp.bfloat16)


def owner_table(placement):
    ident = jnp.arange(placement.shape[0], dtype=jnp.int32)
    hits = placement[None, :] == ident[:, None]
    return jnp.sum(jnp.where(hits, ident[None, :], 0), axis=1)


def reorder_blocks(weights, source, n_dest):
    shape = weights.shape
    blocks = weights.reshape(shape[0], shape[1], n_dest, shape[2] // n_dest)
    return jnp.take(blocks, source, axis=2).reshape(shape)


def build_sends(normed, expert_ids, owner, n_dest, capacity):
    tok_rows, top_count = expert_ids.shape
    experts_all = owner.shape[0]
    expert_hits = expert_ids[:, :, None] == jnp.arange(experts_all, dtype=jnp.int32)[None, None, :]
    destination = jnp.sum(jnp.where(expert_hits, owner[None, None, :], 0), axis=2)
    flat_dest = destination.reshape(-1)
    dest_hits = (flat_dest[:, None] == jnp.arange(n_dest, dtype=jnp.int32)[None, :]).astype(
        jnp.int32
    )
    earlier = jnp.cumsum(dest_hits, axis=0) - dest_hits
    position = jnp.sum(earlier * dest_hits, axis=1)
    slot_index = (flat_dest * capacity + position).reshape(tok_rows, top_count)
    slot_hits = (
        slot_index[:, :, None] == jnp.arange(n_dest * capacity, dtype=jnp.int32)[None, None, :]
    )
    selector = jnp.sum(slot_hits.astype(jnp.float32), axis=1).astype(jnp.bfloat16)
    sends = jnp.einsum("ts,td->sd", selector, normed, preferred_element_type=jnp.float32).astype(
        jnp.bfloat16
    )
    return (sends.reshape(n_dest, capacity, normed.shape[1]), slot_index)


def expert_block(rows, shards):
    gate_part, up_part, down_part = shards
    columns = rows
    gate_vals = jnp.dot(
        columns,
        lax.all_gather(gate_part, "grp", axis=1, tiled=True)[0],
        preferred_element_type=jnp.float32,
    )
    up_vals = jnp.dot(
        columns,
        lax.all_gather(up_part, "grp", axis=1, tiled=True)[0],
        preferred_element_type=jnp.float32,
    )
    hidden = (jax.nn.silu(gate_vals) * up_vals).astype(jnp.bfloat16)
    columns = hidden
    outputs = jnp.dot(
        columns,
        lax.all_gather(down_part, "grp", axis=1, tiled=True)[0],
        preferred_element_type=jnp.float32,
    )
    return outputs.astype(jnp.bfloat16)


def combine_rows(residual_rows, gates, returned_rows, slot_index):
    picked = returned_rows[slot_index].astype(jnp.float32)
    return (residual_rows + jnp.sum(gates[:, :, None] * picked, axis=1)).astype(jnp.bfloat16)


def per_device(
    states,
    route_ids,
    route_gates,
    moe_gain,
    final_gain,
    gate_proj,
    up_proj,
    down_proj,
    old_slots,
    new_slots,
    req_lengths,
    head_proj,
):
    n_dest = lax.axis_size("ep")
    column = lax.axis_index("ep")
    tok_rows = states.shape[1]
    width = states.shape[2]
    top_count = route_ids.shape[2]
    experts_all = old_slots.shape[0]
    capacity = min(tok_rows, max(2, 3 * tok_rows * top_count // (2 * experts_all)))
    old_owner = owner_table(old_slots)
    new_owner = owner_table(new_slots)
    source = jnp.take(old_owner, new_slots)
    spread = (
        lax.all_to_all(gate_proj, "ep", split_axis=2, concat_axis=2, tiled=True),
        lax.all_to_all(up_proj, "ep", split_axis=2, concat_axis=2, tiled=True),
        lax.all_to_all(down_proj, "ep", split_axis=2, concat_axis=2, tiled=True),
    )
    gate_sorted = reorder_blocks(spread[0], source, n_dest)
    up_sorted = reorder_blocks(spread[1], source, n_dest)
    down_sorted = reorder_blocks(spread[2], source, n_dest)
    moved = (
        lax.all_to_all(gate_sorted, "ep", split_axis=2, concat_axis=2, tiled=True),
        lax.all_to_all(up_sorted, "ep", split_axis=2, concat_axis=2, tiled=True),
        lax.all_to_all(down_sorted, "ep", split_axis=2, concat_axis=2, tiled=True),
    )
    moved_gate, moved_up, moved_down = moved
    residual = states.astype(jnp.float32)
    normed = normalize(residual, moe_gain)
    outputs = []
    for batch_index, owner, shards in (
        (0, old_owner, (gate_proj, up_proj, down_proj)),
        (1, new_owner, (moved_gate, moved_up, moved_down)),
    ):
        sends, slot_index = build_sends(
            normed[batch_index], route_ids[batch_index], owner, n_dest, capacity
        )
        arrived = lax.all_to_all(sends, "ep", split_axis=0, concat_axis=0, tiled=True)
        results = expert_block(arrived.reshape(n_dest * capacity, width), shards)
        returned = lax.all_to_all(
            results.reshape(n_dest, capacity, width), "ep", split_axis=0, concat_axis=0, tiled=True
        )
        outputs.append(
            combine_rows(
                residual[batch_index],
                route_gates[batch_index],
                returned.reshape(n_dest * capacity, width),
                slot_index,
            )
        )
    mixed = jnp.stack(outputs)
    request_ends = jnp.cumsum(req_lengths[:, 0, :], axis=-1) - 1
    local_ends = request_ends - column * tok_rows
    picker = (
        local_ends[:, :, None] == jnp.arange(tok_rows, dtype=jnp.int32)[None, None, :]
    ).astype(jnp.bfloat16)
    tail_terms = jnp.einsum("brt,btd->brd", picker, mixed, preferred_element_type=jnp.float32)
    group_tails = lax.psum(tail_terms.astype(jnp.bfloat16), "ep")
    gathered = lax.all_gather(group_tails, "grp", axis=1, tiled=True)
    finals = normalize(gathered.astype(jnp.float32), final_gain)
    logits = jnp.dot(finals.reshape(-1, width), head_proj, preferred_element_type=jnp.float32)
    top_val = lax.pmax(jnp.max(logits, axis=1), ("grp", "ep"))
    totals = lax.psum(jnp.sum(jnp.exp(logits - top_val[:, None]), axis=1), ("grp", "ep"))
    log_probs = (logits - top_val[:, None] - jnp.log(totals)[:, None]).reshape(
        2, -1, logits.shape[1]
    )
    return (mixed, moved_gate, moved_up, moved_down, log_probs)


def solution(mesh):
    placed = (
        P(None, ("grp", "ep"), None),
        P(None, ("grp", "ep"), None),
        P(None, ("grp", "ep"), None),
        P(),
        P(),
        P("ep", "grp", None),
        P("ep", "grp", None),
        P("ep", "grp", None),
        P(),
        P(),
        P(None, "grp", None),
        P(None, ("grp", "ep")),
    )
    return jax.shard_map(
        per_device,
        mesh=mesh,
        in_specs=placed,
        out_specs=(
            P(None, ("grp", "ep"), None),
            P("ep", "grp", None),
            P("ep", "grp", None),
            P("ep", "grp", None),
            P(None, None, ("grp", "ep")),
        ),
        check_vma=False,
    )
```

profile of v0, /device:TPU:0, one launch (start us, length us, event | category | flops | bytes accessed | tf_op | source)
XLA Modules:
  0.0 611.8 jit_solution(1638913436100575654)
XLA Ops:
  7.2 4.7 copy.107
  12.4 7.8 %reduce.6 = bf16[512,1024]{1,0:T(8,128)(2,1)} reduce(bf16[512,1,1024]{2,1,0:T(2,128)(2,1)S(1)} %bitcast.152, bf16[]{:T(256)} %broadcast.285), dimensions={1}, to_apply=%bitcast.118.reduce_sub_computation | reduce | bytes 2097154
  22.9 7.7 %all-to-all-start.3 = ((bf16[16,2,16384]{2,1,0:T(2,128)(2,1)}), bf16[16,2,16384]{2,1,0:T(2,128)(2,1)}, u32[]{:S(2)}, u32[]{:S(2)}) async-start(bf16[16,2,16384]{2,1,0:T(2,128)(2,1)} %reshape.355), calls=%async_computation.3 | async-start | bytes 2097152 | tf_op jit(solution)/shard_map/all_to_all | solution.py:99
  32.6 7.8 %reduce.7 = bf16[512,1024]{1,0:T(8,128)(2,1)} reduce(bf16[512,1,1024]{2,1,0:T(2,128)(2,1)S(1)} %bitcast.156, bf16[]{:T(256)} %broadcast.285), dimensions={1}, to_apply=%bitcast.114.reduce_sub_computation | reduce | bytes 2097154
  40.3 2.7 reshape.351
  43.0 10.5 %all-to-all-done.3 = bf16[16,2,16384]{2,1,0:T(2,128)(2,1)} async-done(((bf16[16,2,16384]{2,1,0:T(2,128)(2,1)}), bf16[16,2,16384]{2,1,0:T(2,128)(2,1)}, u32[]{:S(2)}, u32[]{:S(2)}) %all-to-all-start.3) | async-done | bytes 1048608 | tf_op jit(solution)/shard_map/all_to_all | solution.py:99
  53.5 6.9 %all-to-all-start.5 = ((bf16[16,2,16384]{2,1,0:T(2,128)(2,1)}), bf16[16,2,16384]{2,1,0:T(2,128)(2,1)}, u32[]{:S(2)}, u32[]{:S(2)}) async-start(bf16[16,2,16384]{2,1,0:T(2,128)(2,1)} %reshape.351), calls=%async_computation.5 | async-start | bytes 2097152 | tf_op jit(solution)/shard_map/all_to_all | solution.py:100
  62.7 10.6 %reduce.4 = bf16[2048,256]{1,0:T(8,128)(2,1)S(1)} reduce(bf16[2048,1,256]{2,1,0:T(2,128)(2,1)S(1)} %bitcast.157, bf16[]{:T(256)} %broadcast.285), dimensions={1}, to_apply=%bitcast.110.reduce_sub_computation | reduce | bytes 2097154
  74.4 9.0 %all-to-all-done.5 = bf16[16,2,16384]{2,1,0:T(2,128)(2,1)} async-done(((bf16[16,2,16384]{2,1,0:T(2,128)(2,1)}), bf16[16,2,16384]{2,1,0:T(2,128)(2,1)}, u32[]{:S(2)}, u32[]{:S(2)}) %all-to-all-start.5) | async-done | bytes 1048608 | tf_op jit(solution)/shard_map/all_to_all | solution.py:100
  83.5 7.3 %all-to-all-start.7 = ((bf16[16,2,16384]{2,1,0:T(2,128)(2,1)}), bf16[16,2,16384]{2,1,0:T(2,128)(2,1)S(1)}, u32[]{:S(2)}, u32[]{:S(2)}) async-start(bf16[16,2,16384]{2,1,0:T(2,128)(2,1)} %reshape.347), calls=%async_computation.7 | async-start | bytes 2097152 | tf_op jit(solution)/shard_map/all_to_all | solution.py:101
  95.9 17.7 %all-to-all-done.7 = bf16[16,2,16384]{2,1,0:T(2,128)(2,1)S(1)} async-done(((bf16[16,2,16384]{2,1,0:T(2,128)(2,1)}), bf16[16,2,16384]{2,1,0:T(2,128)(2,1)S(1)}, u32[]{:S(2)}, u32[]{:S(2)}) %all-to-all-start.7) | async-done | bytes 1048608 | tf_op jit(solution)/shard_map/all_to_all | solution.py:101
  114.6 6.9 %all-to-all-start.2 = ((bf16[16,30,2048]{2,1,0:T(8,128)(2,1)}), bf16[16,30,2048]{2,1,0:T(8,128)(2,1)S(1)}, u32[]{:S(2)}, u32[]{:S(2)}) async-start(bf16[16,30,2048]{2,1,0:T(8,128)(2,1)} %reshape.258), calls=%async_computation.2 | async-start | bytes 4194304 | tf_op jit(solution)/shard_map/all_to_all | solution.py:122
  123.5 2.9 convolution_convert_fusion.3
  126.3 2.9 reshape.252
  129.2 33.4 %all-to-all-done.2 = bf16[16,30,2048]{2,1,0:T(8,128)(2,1)S(1)} async-done(((bf16[16,30,2048]{2,1,0:T(8,128)(2,1)}), bf16[16,30,2048]{2,1,0:T(8,128)(2,1)S(1)}, u32[]{:S(2)}, u32[]{:S(2)}) %all-to-all-start.2) | async-done | bytes 1966112 | tf_op jit(solution)/shard_map/all_to_all | solution.py:122
  164.0 11.3 %all-to-all-start = ((bf16[16,30,2048]{2,1,0:T(8,128)(2,1)}), bf16[16,30,2048]{2,1,0:T(8,128)(2,1)}, u32[]{:S(2)}, u32[]{:S(2)}) async-start(bf16[16,30,2048]{2,1,0:T(8,128)(2,1)} %reshape.252), calls=%async_computation | async-start | bytes 4194304 | tf_op jit(solution)/shard_map/all_to_all | solution.py:122
  177.4 4.3 reshape.356
  182.1 5.9 reshape.352
  193.2 7.8 %reduce.9 = bf16[512,1024]{1,0:T(8,128)(2,1)} reduce(bf16[512,1,1024]{2,1,0:T(2,128)(2,1)S(1)} %bitcast.154, bf16[]{:T(256)} %broadcast.285), dimensions={1}, to_apply=%bitcast.141.reduce_sub_computation | reduce | bytes 2097154
  203.6 12.8 %all-to-all-done = bf16[16,30,2048]{2,1,0:T(8,128)(2,1)} async-done(((bf16[16,30,2048]{2,1,0:T(8,128)(2,1)}), bf16[16,30,2048]{2,1,0:T(8,128)(2,1)}, u32[]{:S(2)}, u32[]{:S(2)}) %all-to-all-start) | async-done | bytes 1966112 | tf_op jit(solution)/shard_map/all_to_all | solution.py:122
  216.4 11.3 %all-to-all-start.4 = ((bf16[16,2,16384]{2,1,0:T(2,128)(2,1)}), bf16[16,2,16384]{2,1,0:T(2,128)(2,1)}, u32[]{:S(2)}, u32[]{:S(2)}) async-start(bf16[16,2,16384]{2,1,0:T(2,128)(2,1)} %reshape.357), calls=%async_computation.4 | async-start | bytes 2097152 | tf_op jit(solution)/shard_map/all_to_all | solution.py:107
  230.0 6.8 %reduce.8 = bf16[512,1024]{1,0:T(8,128)(2,1)S(1)} reduce(bf16[512,1,1024]{2,1,0:T(2,128)(2,1)S(1)} %bitcast.155, bf16[]{:T(256)} %broadcast.285), dimensions={1}, to_apply=%bitcast.140.reduce_sub_computation | reduce | bytes 2097154
  238.4 12.2 %all-to-all-done.4 = bf16[16,2,16384]{2,1,0:T(2,128)(2,1)} async-done(((bf16[16,2,16384]{2,1,0:T(2,128)(2,1)}), bf16[16,2,16384]{2,1,0:T(2,128)(2,1)}, u32[]{:S(2)}, u32[]{:S(2)}) %all-to-all-start.4) | async-done | bytes 1048608 | tf_op jit(solution)/shard_map/all_to_all | solution.py:107
  250.7 6.9 %all-to-all-start.6 = ((bf16[16,2,16384]{2,1,0:T(2,128)(2,1)}), bf16[16,2,16384]{2,1,0:T(2,128)(2,1)}, u32[]{:S(2)}, u32[]{:S(2)}) async-start(bf16[16,2,16384]{2,1,0:T(2,128)(2,1)} %reshape.353), calls=%async_computation.6 | async-start | bytes 2097152 | tf_op jit(solution)/shard_map/all_to_all | solution.py:108
  257.8 4.3 reshape.358
  262.2 4.2 copy.109
  270.3 11.7 %copy.146 = bf16[1,256,2048]{1,0,2:T(2,128)(2,1)S(1)} copy(bf16[1,256,2048]{1,2,0:T(8,128)(2,1)S(1)} %bitcast_select_fusion.2) | data formatting | bytes 2097152 | tf_op jit(solution)/shard_map/jit(_take)/select_n | solution.py:21
  282.0 10.6 %reduce.5 = bf16[2048,256]{1,0:T(8,128)(2,1)S(1)} reduce(bf16[2048,1,256]{2,1,0:T(2,128)(2,1)S(1)} %bitcast.153, bf16[]{:T(256)} %broadcast.285), dimensions={1}, to_apply=%bitcast.139.reduce_sub_computation | reduce | bytes 2097154
  293.7 6.0 all-to-all-start.8
  299.7 4.3 reshape.354
  304.1 4.2 copy.112
  310.2 3.7 fusion.10
  313.9 6.1 convolution_convert_fusion.2
  320.0 2.8 reshape.254
  322.8 6.7 %all-to-all-start.1 = ((bf16[16,30,2048]{2,1,0:T(8,128)(2,1)}), bf16[16,30,2048]{2,1,0:T(8,128)(2,1)}, u32[]{:S(2)}, u32[]{:S(2)}) async-start(bf16[16,30,2048]{2,1,0:T(8,128)(2,1)} %reshape.254), calls=%async_computation.1 | async-start | bytes 4194304 | tf_op jit(solution)/shard_map/all_to_all | solution.py:124
  330.9 4.2 copy.117
  337.0 2.8 fusion.5
  339.8 11.9 %all-gather.15.cloned.1.call-done = bf16[1,2048,512]{2,1,0:T(8,128)(2,1)} async-done(((bf16[1,1024,512]{2,1,0:T(8,128)(2,1)}), bf16[1,2048,512]{2,1,0:T(8,128)(2,1)}) %all-gather.15.cloned.1.call-update) | async-done | bytes 2097168 | tf_op jit(solution)/shard_map/all_gather | solution.py:56
  351.7 35.1 %all-gather.17.cloned.1.call-done = bf16[1,512,2048]{2,1,0:T(8,128)(2,1)} async-done(((bf16[1,256,2048]{2,1,0:T(8,128)(2,1)}), bf16[1,512,2048]{2,1,0:T(8,128)(2,1)}) %all-gather.17.cloned.1.call-update) | async-done | bytes 2097168 | tf_op jit(solution)/shard_map/all_gather | solution.py:63
  386.8 5.9 convolution_convert_fusion
  392.7 2.8 reshape.265
  395.5 5.8 all-to-all-start.9
  409.5 32.9 %all-to-all-done.9 = bf16[16,30,2048]{2,1,0:T(8,128)(2,1)} async-done(((bf16[16,30,2048]{2,1,0:T(8,128)(2,1)}), bf16[16,30,2048]{2,1,0:T(8,128)(2,1)}, u32[]{:S(2)}, u32[]{:S(2)}) %all-to-all-start.9) | async-done | bytes 1966112 | tf_op jit(solution)/shard_map/all_to_all | solution.py:124
  449.4 67.3 %psum.14 = bf16[2,4,2048]{2,1,0:T(4,128)(2,1)S(1)} all-reduce(bf16[2,4,2048]{2,1,0:T(4,128)(2,1)S(1)} %convolution_convert_fusion.4), channel_id=1, replica_groups=mesh['grp'=2,'ep'=16] {'ep'}, use_global_device_ids=true, to_apply=%region_16.18 | all-reduce | flops 16384 | bytes 65536 | tf_op jit(solution)/shard_map/psum | solution.py:142
  516.7 4.6 all_gather.27
  521.4 3.9 fusion.50
  525.3 36.9 %pmax.7 = f32[16]{0:T(128)S(1)} all-reduce(f32[16]{0:T(128)S(1)} %get-tuple-element.41), channel_id=1, replica_groups=mesh['grp'=2,'ep'=16] {'grp','ep'}, use_global_device_ids=true, to_apply=%region_19.21 | all-reduce | flops 16 | bytes 128 | tf_op jit(solution)/shard_map/pmax | solution.py:146
  562.4 41.4 %psum.15 = f32[16]{0:T(128)S(1)} all-reduce(f32[16]{0:T(128)S(1)} %exponential_reduce_fusion), channel_id=1, replica_groups=mesh['grp'=2,'ep'=16] {'grp','ep'}, use_global_device_ids=true, to_apply=%region_21.23 | all-reduce | flops 16 | bytes 128 | tf_op jit(solution)/shard_map/psum | solution.py:147
  (151 shorter events, 58.5 us)
Async XLA Ops:
  20.2 10.4 %copy-start.2 = (bf16[1,1024,512]{2,1,0:T(8,128)(2,1)S(1)}, bf16[1,1024,512]{2,1,0:T(8,128)(2,1)}, u32[]{:S(2)}) copy-start(bf16[1,1024,512]{2,1,0:T(8,128)(2,1)} %param.20) | copy-start | bytes 3145732
  22.9 30.6 %all-to-all-start.3 = ((bf16[16,2,16384]{2,1,0:T(2,128)(2,1)}), bf16[16,2,16384]{2,1,0:T(2,128)(2,1)}, u32[]{:S(2)}, u32[]{:S(2)}) async-start(bf16[16,2,16384]{2,1,0:T(2,128)(2,1)} %reshape.355), calls=%async_computation.3 | async-start | bytes 2097152 | tf_op jit(solution)/shard_map/all_to_all | solution.py:99
  40.3 20.1 %copy-start.15 = (s32[16]{0:T(128)S(1)}, s32[16]{0:T(128)}, u32[]{:S(2)}) copy-start(s32[16]{0:T(128)} %param.22) | copy-start | bytes 196
  40.3 20.3 %copy-start.14 = (s32[16]{0:T(128)S(1)}, s32[16]{0:T(128)}, u32[]{:S(2)}) copy-start(s32[16]{0:T(128)} %param.23) | copy-start | bytes 196
  40.3 20.4 %copy-start.10 = (s32[2,40,8]{1,2,0:T(8,128)S(1)}, s32[2,40,8]{1,2,0:T(8,128)}, u32[]{:S(2)}) copy-start(s32[2,40,8]{1,2,0:T(8,128)} %param.15) | copy-start | bytes 7684
  40.3 20.7 %copy-start.1 = (bf16[1,256,2048]{2,1,0:T(8,128)(2,1)S(1)}, bf16[1,256,2048]{2,1,0:T(8,128)(2,1)}, u32[]{:S(2)}) copy-start(bf16[1,256,2048]{2,1,0:T(8,128)(2,1)} %param.21) | copy-start | bytes 3145732
  53.5 29.9 %all-to-all-start.5 = ((bf16[16,2,16384]{2,1,0:T(2,128)(2,1)}), bf16[16,2,16384]{2,1,0:T(2,128)(2,1)}, u32[]{:S(2)}, u32[]{:S(2)}) async-start(bf16[16,2,16384]{2,1,0:T(2,128)(2,1)} %reshape.351), calls=%async_computation.5 | async-start | bytes 2097152 | tf_op jit(solution)/shard_map/all_to_all | solution.py:100
  73.3 19.2 %copy-start.5 = (bf16[2,40,2048]{2,1,0:T(8,128)(2,1)S(1)}, bf16[2,40,2048]{2,1,0:T(8,128)(2,1)}, u32[]{:S(2)}) copy-start(bf16[2,40,2048]{2,1,0:T(8,128)(2,1)} %param.14) | copy-start | bytes 983044
  73.3 19.4 %copy-start.12 = (f32[2048]{0:T(1024)S(1)}, f32[2048]{0:T(1024)}, u32[]{:S(2)}) copy-start(f32[2048]{0:T(1024)} %param.17) | copy-start | bytes 24580
  83.5 30.2 %all-to-all-start.7 = ((bf16[16,2,16384]{2,1,0:T(2,128)(2,1)}), bf16[16,2,16384]{2,1,0:T(2,128)(2,1)S(1)}, u32[]{:S(2)}, u32[]{:S(2)}) async-start(bf16[16,2,16384]{2,1,0:T(2,128)(2,1)} %reshape.347), calls=%async_computation.7 | async-start | bytes 2097152 | tf_op jit(solution)/shard_map/all_to_all | solution.py:101
  92.8 0.7 copy-start.7
  113.6 1.0 copy-start.3
  114.6 48.0 %all-to-all-start.2 = ((bf16[16,30,2048]{2,1,0:T(8,128)(2,1)}), bf16[16,30,2048]{2,1,0:T(8,128)(2,1)S(1)}, u32[]{:S(2)}, u32[]{:S(2)}) async-start(bf16[16,30,2048]{2,1,0:T(8,128)(2,1)} %reshape.258), calls=%async_computation.2 | async-start | bytes 4194304 | tf_op jit(solution)/shard_map/all_to_all | solution.py:122
  162.6 1.4 copy-start
  164.0 52.4 %all-to-all-start = ((bf16[16,30,2048]{2,1,0:T(8,128)(2,1)}), bf16[16,30,2048]{2,1,0:T(8,128)(2,1)}, u32[]{:S(2)}, u32[]{:S(2)}) async-start(bf16[16,30,2048]{2,1,0:T(8,128)(2,1)} %reshape.252), calls=%async_computation | async-start | bytes 4194304 | tf_op jit(solution)/shard_map/all_to_all | solution.py:122
  175.2 134.9 %all-gather.7.cloned.1.call-start = ((), (), s32[]{:S(2)}) async-start(), calls=%async_computation.10 | async-start | bytes 3145728 | tf_op jit(solution)/shard_map/all_gather | solution.py:51
  176.0 137.9 %all-gather.11.cloned.1.call-start = ((), (), s32[]{:S(2)}) async-start(), calls=%async_computation.12 | async-start | bytes 3145728 | tf_op jit(solution)/shard_map/all_gather | solution.py:63
  216.4 34.3 %all-to-all-start.4 = ((bf16[16,2,16384]{2,1,0:T(2,128)(2,1)}), bf16[16,2,16384]{2,1,0:T(2,128)(2,1)}, u32[]{:S(2)}, u32[]{:S(2)}) async-start(bf16[16,2,16384]{2,1,0:T(2,128)(2,1)} %reshape.357), calls=%async_computation.4 | async-start | bytes 2097152 | tf_op jit(solution)/shard_map/all_to_all | solution.py:107
  227.7 86.2 %all-gather.9.cloned.1.call-start = ((), (), s32[]{:S(2)}) async-start(), calls=%async_computation.11 | async-start | bytes 3145728 | tf_op jit(solution)/shard_map/all_gather | solution.py:56
  250.7 43.1 %all-to-all-start.6 = ((bf16[16,2,16384]{2,1,0:T(2,128)(2,1)}), bf16[16,2,16384]{2,1,0:T(2,128)(2,1)}, u32[]{:S(2)}, u32[]{:S(2)}) async-start(bf16[16,2,16384]{2,1,0:T(2,128)(2,1)} %reshape.353), calls=%async_computation.6 | async-start | bytes 2097152 | tf_op jit(solution)/shard_map/all_to_all | solution.py:108
  257.6 79.4 %all-gather.13.cloned.1.call-start = ((), (), s32[]{:S(2)}) async-start(), calls=%async_computation.13 | async-start | bytes 3145728 | tf_op jit(solution)/shard_map/all_gather | solution.py:51
  262.2 4.3 copy-start.4
  293.7 29.1 %all-to-all-start.8 = ((bf16[16,2,16384]{2,1,0:T(2,128)(2,1)}), bf16[16,2,16384]{2,1,0:T(2,128)(2,1)S(1)}, u32[]{:S(2)}, u32[]{:S(2)}) async-start(bf16[16,2,16384]{2,1,0:T(2,128)(2,1)} %reshape.349), calls=%async_computation.8 | async-start | bytes 2097152 | tf_op jit(solution)/shard_map/all_to_all | solution.py:109
  299.7 52.0 %all-gather.15.cloned.1.call-start = ((), (), s32[]{:S(2)}) async-start(), calls=%async_computation.14 | async-start | bytes 3145728 | tf_op jit(solution)/shard_map/all_gather | solution.py:56
  322.8 72.7 %all-to-all-start.1 = ((bf16[16,30,2048]{2,1,0:T(8,128)(2,1)}), bf16[16,30,2048]{2,1,0:T(8,128)(2,1)}, u32[]{:S(2)}, u32[]{:S(2)}) async-start(bf16[16,30,2048]{2,1,0:T(8,128)(2,1)} %reshape.254), calls=%async_computation.1 | async-start | bytes 4194304 | tf_op jit(solution)/shard_map/all_to_all | solution.py:124
  329.6 57.2 %all-gather.17.cloned.1.call-start = ((), (), s32[]{:S(2)}) async-start(), calls=%async_computation.15 | async-start | bytes 3145728 | tf_op jit(solution)/shard_map/all_gather | solution.py:63
  395.5 7.2 %copy-start.11 = (f32[2,40,8]{1,2,0:T(8,128)S(1)}, f32[2,40,8]{1,2,0:T(8,128)}, u32[]{:S(2)}) copy-start(f32[2,40,8]{1,2,0:T(8,128)} %param.16) | copy-start | bytes 7684
  395.5 7.6 %copy-start.13 = (s32[2,1,4]{2,1,0:T(1,128)S(1)}, s32[2,1,4]{2,1,0:T(1,128)}, u32[]{:S(2)}) copy-start(s32[2,1,4]{2,1,0:T(1,128)} %param.24) | copy-start | bytes 100
  395.5 47.0 %all-to-all-start.9 = ((bf16[16,30,2048]{2,1,0:T(8,128)(2,1)}), bf16[16,30,2048]{2,1,0:T(8,128)(2,1)}, u32[]{:S(2)}, u32[]{:S(2)}) async-start(bf16[16,30,2048]{2,1,0:T(8,128)(2,1)} %reshape.265), calls=%async_computation.9 | async-start | bytes 4194304 | tf_op jit(solution)/shard_map/all_to_all | solution.py:124
  446.7 1.3 copy-start.6
  446.7 74.6 %copy-start.9 = (f32[2048]{0:T(1024)S(1)}, f32[2048]{0:T(1024)}, u32[]{:S(2)}) copy-start(f32[2048]{0:T(1024)} %param.18) | copy-start | bytes 24580
  449.1 76.1 %copy-start.8 = (bf16[2,40,2048]{2,1,0:T(8,128)(2,1)}, bf16[2,40,2048]{2,1,0:T(8,128)(2,1)S(1)}, u32[]{:S(2)}) copy-start(bf16[2,40,2048]{2,1,0:T(8,128)(2,1)S(1)} %pad_maximum_fusion) | copy-start | bytes 983044
Sparse Core Ops, SparseCore 0:
  177.6 34.3 all-gather.6
  213.6 33.1 all-gather.10
  248.3 33.1 all-gather.8
  283.4 33.1 all-gather.12
  318.5 33.1 all-gather.14
  353.6 33.1 all-gather.16
where the time goes:
time: 619 us; the launch traced here: 612 us
  waiting for transfers between devices  178 us (29%)
  blocking collectives  150 us (24%)
  local copies, waits for them, and re-layouts  103 us (17%)
  starting transfers between devices  77.6 us (13%)
  other arithmetic  61.8 us (10%)
  matrix products  26.1 us (4%)
  between operations  15.2 us (2%)
    psum x1, blocking collectives, per_device(): group_tails = lax.psum(tail_terms.astype(jnp.bfloat16), 'ep')  67.3 us
    unnamed x6, other arithmetic  51.2 us
    unnamed x51, local copies, waits for them, and re-layouts  47.4 us
    all_to_all x2, waiting for transfers between devices, per_device(): lax.all_to_all(sends, 'ep', split_axis=0, concat_axis=0, tiled=True)  46.2 us
    psum x1, blocking collectives, per_device(): lax.psum(jnp.sum(jnp.exp(logits - top_val[:, None]), axis=1), ('grp', 'ep'))  41.4 us
    pmax x1, blocking collectives, per_device(): top_val = lax.pmax(jnp.max(logits, axis=1), ('grp', 'ep'))  36.9 us
    all_gather x2, waiting for transfers between devices, expert_block(): lax.all_gather(down_part, 'grp', axis=1, tiled=True)[0]  35.1 us
    all_to_all x2, waiting for transfers between devices, per_device(): lax.all_to_all(results.reshape(n_dest, capacity, width), 'ep', split_axis...  32.9 us
  transfers between devices with their start and end apart: 16, of which 9 were waited for; matrix products, arithmetic and copies ran while one was open for 26% of the time, Pallas kernels for 0%

commit v1 on v0

--- a/solution.py
+++ b/solution.py
@@ -104,7 +104,12 @@
     up_sorted = reorder_blocks(spread[1], source, n_dest)
     down_sorted = reorder_blocks(spread[2], source, n_dest)
     moved = (
-        lax.all_to_all(gate_sorted, "ep", split_axis=2, concat_axis=2, tiled=True),
+        jnp.concatenate(
+            lax.all_to_all(
+                jnp.stack(jnp.split(gate_sorted, lax.axis_size("ep"), axis=2)), "ep", 0, 0
+            ),
+            axis=2,
+        ),
         lax.all_to_all(up_sorted, "ep", split_axis=2, concat_axis=2, tiled=True),
         lax.all_to_all(down_sorted, "ep", split_axis=2, concat_axis=2, tiled=True),
     )

time: 619 us -> 602 us (0.973)
  waiting for transfers between devices: 178 us -> 168 us
    all_gather x2, waiting for transfers between devices: 11.9 us -> 3.3 us  [expert_block(): lax.all_gather(up_part, 'grp', axis=1, tiled=True)[0]]
    unnamed x6 -> x5, other arithmetic: 51.2 us -> 43.5 us
    unnamed x51 -> x65, local copies, waits for them, and re-layouts: 47.4 us -> 52.1 us
where the time goes in v1:
time: 602 us; the launch traced here: 595 us
  waiting for transfers between devices  168 us (28%)
  blocking collectives  150 us (25%)
  local copies, waits for them, and re-layouts  103 us (17%)
  starting transfers between devices  76.9 us (13%)
  other arithmetic  55.7 us (9%)
  matrix products  26.1 us (4%)
  between operations  14.9 us (2%)
    psum x1, blocking collectives, per_device(): group_tails = lax.psum(tail_terms.astype(jnp.bfloat16), 'ep')  67.3 us
    unnamed x65, local copies, waits for them, and re-layouts  52.1 us
    all_to_all x2, waiting for transfers between devices, per_device(): lax.all_to_all(sends, 'ep', split_axis=0, concat_axis=0, tiled=True)  47.4 us
    unnamed x5, other arithmetic  43.5 us
    psum x1, blocking collectives, per_device(): lax.psum(jnp.sum(jnp.exp(logits - top_val[:, None]), axis=1), ('grp', 'ep'))  41.4 us
    pmax x1, blocking collectives, per_device(): top_val = lax.pmax(jnp.max(logits, axis=1), ('grp', 'ep'))  36.9 us
    all_gather x2, waiting for transfers between devices, expert_block(): lax.all_gather(down_part, 'grp', axis=1, tiled=True)[0]  35.1 us
    all_to_all x2, waiting for transfers between devices, per_device(): lax.all_to_all(results.reshape(n_dest, capacity, width), 'ep', split_axis...  33 us
  transfers between devices with their start and end apart: 16, of which 9 were waited for; matrix products, arithmetic and copies ran while one was open for 26% of the time, Pallas kernels for 0%

profile of v1, /device:TPU:0, one launch (start us, length us, event | category | flops | bytes accessed | tf_op | source)
XLA Modules:
  0.0 594.6 jit_solution(2639254218357375186)
XLA Ops:
  7.2 4.7 copy.119
  12.4 7.8 %reduce.6 = bf16[512,1024]{1,0:T(8,128)(2,1)} reduce(bf16[512,1,1024]{2,1,0:T(2,128)(2,1)S(1)} %bitcast.216, bf16[]{:T(256)} %broadcast.285), dimensions={1}, to_apply=%bitcast.185.reduce_sub_computation | reduce | bytes 2097154
  20.2 2.7 reshape.363
  22.9 7.6 %all-to-all-start.3 = ((bf16[16,2,16384]{2,1,0:T(2,128)(2,1)}), bf16[16,2,16384]{2,1,0:T(2,128)(2,1)}, u32[]{:S(2)}, u32[]{:S(2)}) async-start(bf16[16,2,16384]{2,1,0:T(2,128)(2,1)} %reshape.363), calls=%async_computation.3 | async-start | bytes 2097152 | tf_op jit(solution)/shard_map/all_to_all | solution.py:99
  32.5 6.8 %reduce.7 = bf16[512,1024]{1,0:T(8,128)(2,1)S(1)} reduce(bf16[512,1,1024]{2,1,0:T(2,128)(2,1)S(1)} %bitcast.219, bf16[]{:T(256)} %broadcast.285), dimensions={1}, to_apply=%bitcast.181.reduce_sub_computation | reduce | bytes 2097154
  40.9 12.6 %all-to-all-done.3 = bf16[16,2,16384]{2,1,0:T(2,128)(2,1)} async-done(((bf16[16,2,16384]{2,1,0:T(2,128)(2,1)}), bf16[16,2,16384]{2,1,0:T(2,128)(2,1)}, u32[]{:S(2)}, u32[]{:S(2)}) %all-to-all-start.3) | async-done | bytes 1048608 | tf_op jit(solution)/shard_map/all_to_all | solution.py:99
  53.5 6.9 %all-to-all-start.5 = ((bf16[16,2,16384]{2,1,0:T(2,128)(2,1)}), bf16[16,2,16384]{2,1,0:T(2,128)(2,1)}, u32[]{:S(2)}, u32[]{:S(2)}) async-start(bf16[16,2,16384]{2,1,0:T(2,128)(2,1)} %reshape.359), calls=%async_computation.5 | async-start | bytes 2097152 | tf_op jit(solution)/shard_map/all_to_all | solution.py:100
  63.4 10.6 %reduce.4 = bf16[2048,256]{1,0:T(8,128)(2,1)S(1)} reduce(bf16[2048,1,256]{2,1,0:T(2,128)(2,1)S(1)} %bitcast.220, bf16[]{:T(256)} %broadcast.285), dimensions={1}, to_apply=%bitcast.177.reduce_sub_computation | reduce | bytes 2097154
  75.1 8.3 %all-to-all-done.5 = bf16[16,2,16384]{2,1,0:T(2,128)(2,1)} async-done(((bf16[16,2,16384]{2,1,0:T(2,128)(2,1)}), bf16[16,2,16384]{2,1,0:T(2,128)(2,1)}, u32[]{:S(2)}, u32[]{:S(2)}) %all-to-all-start.5) | async-done | bytes 1048608 | tf_op jit(solution)/shard_map/all_to_all | solution.py:100
  83.4 7.3 %all-to-all-start.7 = ((bf16[16,2,16384]{2,1,0:T(2,128)(2,1)}), bf16[16,2,16384]{2,1,0:T(2,128)(2,1)S(1)}, u32[]{:S(2)}, u32[]{:S(2)}) async-start(bf16[16,2,16384]{2,1,0:T(2,128)(2,1)} %reshape.355), calls=%async_computation.7 | async-start | bytes 2097152 | tf_op jit(solution)/shard_map/all_to_all | solution.py:101
  96.8 16.8 %all-to-all-done.7 = bf16[16,2,16384]{2,1,0:T(2,128)(2,1)S(1)} async-done(((bf16[16,2,16384]{2,1,0:T(2,128)(2,1)}), bf16[16,2,16384]{2,1,0:T(2,128)(2,1)S(1)}, u32[]{:S(2)}, u32[]{:S(2)}) %all-to-all-start.7) | async-done | bytes 1048608 | tf_op jit(solution)/shard_map/all_to_all | solution.py:101
  114.6 6.9 %all-to-all-start.2 = ((bf16[16,30,2048]{2,1,0:T(8,128)(2,1)}), bf16[16,30,2048]{2,1,0:T(8,128)(2,1)}, u32[]{:S(2)}, u32[]{:S(2)}) async-start(bf16[16,30,2048]{2,1,0:T(8,128)(2,1)} %reshape.264), calls=%async_computation.2 | async-start | bytes 4194304 | tf_op jit(solution)/shard_map/all_to_all | solution.py:127
  128.2 5.9 reshape.364
  134.1 2.1 copy.135
  136.2 5.8 reshape.360
  145.3 17.4 %all-to-all-done.2 = bf16[16,30,2048]{2,1,0:T(8,128)(2,1)} async-done(((bf16[16,30,2048]{2,1,0:T(8,128)(2,1)}), bf16[16,30,2048]{2,1,0:T(8,128)(2,1)}, u32[]{:S(2)}, u32[]{:S(2)}) %all-to-all-start.2) | async-done | bytes 1966112 | tf_op jit(solution)/shard_map/all_to_all | solution.py:127
  162.7 11.3 %all-to-all-start = ((bf16[16,30,2048]{2,1,0:T(8,128)(2,1)}), bf16[16,30,2048]{2,1,0:T(8,128)(2,1)}, u32[]{:S(2)}, u32[]{:S(2)}) async-start(bf16[16,30,2048]{2,1,0:T(8,128)(2,1)} %reshape.258), calls=%async_computation | async-start | bytes 4194304 | tf_op jit(solution)/shard_map/all_to_all | solution.py:127
  185.1 30.0 %all-to-all-done = bf16[16,30,2048]{2,1,0:T(8,128)(2,1)} async-done(((bf16[16,30,2048]{2,1,0:T(8,128)(2,1)}), bf16[16,30,2048]{2,1,0:T(8,128)(2,1)}, u32[]{:S(2)}, u32[]{:S(2)}) %all-to-all-start) | async-done | bytes 1966112 | tf_op jit(solution)/shard_map/all_to_all | solution.py:127
  215.1 11.2 %all-to-all-start.4 = ((bf16[16,1,1024,32]{2,3,1,0:T(8,128)(2,1)}), bf16[16,1,1024,32]{2,3,1,0:T(8,128)(2,1)S(1)}, u32[]{:S(2)}, u32[]{:S(2)}) async-start(bf16[16,1,1024,32]{2,3,1,0:T(8,128)(2,1)} %fusion.38), calls=%async_computation.4 | async-start | bytes 2097152 | tf_op jit(solution)/shard_map/all_to_all | solution.py:108
  227.1 2.8 copy.156
  229.9 7.8 %reduce.8 = bf16[512,1024]{1,0:T(8,128)(2,1)} reduce(bf16[512,1,1024]{2,1,0:T(2,128)(2,1)S(1)} %bitcast.218, bf16[]{:T(256)} %broadcast.285), dimensions={1}, to_apply=%bitcast.204.reduce_sub_computation | reduce | bytes 2097154
  237.7 2.6 reshape.361
  240.3 9.0 %all-to-all-done.4 = bf16[16,1,1024,32]{2,3,1,0:T(8,128)(2,1)S(1)} async-done(((bf16[16,1,1024,32]{2,3,1,0:T(8,128)(2,1)}), bf16[16,1,1024,32]{2,3,1,0:T(8,128)(2,1)S(1)}, u32[]{:S(2)}, u32[]{:S(2)}) %all-to-all-start.4) | async-done | bytes 1048608 | tf_op jit(solution)/shard_map/all_to_all | solution.py:108
  249.3 6.9 %all-to-all-start.6 = ((bf16[16,2,16384]{2,1,0:T(2,128)(2,1)}), bf16[16,2,16384]{2,1,0:T(2,128)(2,1)}, u32[]{:S(2)}, u32[]{:S(2)}) async-start(bf16[16,2,16384]{2,1,0:T(2,128)(2,1)} %reshape.361), calls=%async_computation.6 | async-start | bytes 2097152 | tf_op jit(solution)/shard_map/all_to_all | solution.py:113
  260.6 11.7 %copy.155 = bf16[1,256,2048]{1,0,2:T(2,128)(2,1)S(1)} copy(bf16[1,256,2048]{1,2,0:T(8,128)(2,1)S(1)} %bitcast_select_fusion.2) | data formatting | bytes 2097152 | tf_op jit(solution)/shard_map/jit(_take)/select_n | solution.py:21
  272.4 10.6 %reduce.5 = bf16[2048,256]{1,0:T(8,128)(2,1)S(1)} reduce(bf16[2048,1,256]{2,1,0:T(2,128)(2,1)S(1)} %bitcast.217, bf16[]{:T(256)} %broadcast.285), dimensions={1}, to_apply=%bitcast.203.reduce_sub_computation | reduce | bytes 2097154
  284.1 6.0 %all-to-all-start.8 = ((bf16[16,2,16384]{2,1,0:T(2,128)(2,1)}), bf16[16,2,16384]{2,1,0:T(2,128)(2,1)S(1)}, u32[]{:S(2)}, u32[]{:S(2)}) async-start(bf16[16,2,16384]{2,1,0:T(2,128)(2,1)} %reshape.357), calls=%async_computation.8 | async-start | bytes 2097152 | tf_op jit(solution)/shard_map/all_to_all | solution.py:114
  290.1 4.3 reshape.362
  294.4 4.2 copy.122
  300.5 3.7 fusion.10
  304.2 6.4 %convolution_convert_fusion.2 = bf16[480,2048]{1,0:T(8,128)(2,1)} fusion(bf16[1,512,2048]{2,1,0:T(8,128)(2,1)} %all-gather.11.cloned.1.call-done, bf16[480,2048]{1,0:T(8,128)(2,1)S(1)} %reshape.259, bf16[1,2048,512]{2,1,0:T(8,128)(2,1)} %all-gather.9.cloned.1.call-done, f32[480,512]{1,0:T(8,128)} %fusion.10), kind=kOutput, calls=%fused_computation.8 | convolution fusion | flops 2015723520 | bytes 9109504 | tf_op jit(solution)/shard_map/dot_general | solution.py:61
  310.6 2.8 reshape.260
  313.4 6.5 %all-to-all-start.1 = ((bf16[16,30,2048]{2,1,0:T(8,128)(2,1)}), bf16[16,30,2048]{2,1,0:T(8,128)(2,1)}, u32[]{:S(2)}, u32[]{:S(2)}) async-start(bf16[16,30,2048]{2,1,0:T(8,128)(2,1)} %reshape.260), calls=%async_computation.1 | async-start | bytes 4194304 | tf_op jit(solution)/shard_map/all_to_all | solution.py:129
  321.0 4.2 copy.127
  327.1 2.8 fusion.5
  329.9 3.3 all-gather.15.cloned.1.call-done
  333.2 35.1 %all-gather.17.cloned.1.call-done = bf16[1,512,2048]{2,1,0:T(8,128)(2,1)} async-done(((bf16[1,256,2048]{2,1,0:T(8,128)(2,1)}), bf16[1,512,2048]{2,1,0:T(8,128)(2,1)}) %all-gather.17.cloned.1.call-update) | async-done | bytes 2097168 | tf_op jit(solution)/shard_map/all_gather | solution.py:63
  368.4 5.9 convolution_convert_fusion
  374.2 2.8 reshape.273
  377.1 5.9 all-to-all-start.9
  386.8 2.4 gather_fusion
  391.2 33.0 %all-to-all-done.9 = bf16[16,30,2048]{2,1,0:T(8,128)(2,1)} async-done(((bf16[16,30,2048]{2,1,0:T(8,128)(2,1)}), bf16[16,30,2048]{2,1,0:T(8,128)(2,1)}, u32[]{:S(2)}, u32[]{:S(2)}) %all-to-all-start.9) | async-done | bytes 1966112 | tf_op jit(solution)/shard_map/all_to_all | solution.py:129
  425.9 2.4 gather_fusion.3
  431.0 67.3 %psum.14 = bf16[2,4,2048]{2,1,0:T(4,128)(2,1)S(1)} all-reduce(bf16[2,4,2048]{2,1,0:T(4,128)(2,1)S(1)} %convolution_convert_fusion.4), channel_id=1, replica_groups=mesh['grp'=2,'ep'=16] {'ep'}, use_global_device_ids=true, to_apply=%region_16.18 | all-reduce | flops 16384 | bytes 65536 | tf_op jit(solution)/shard_map/psum | solution.py:147
  498.3 4.6 all_gather.27
  503.1 4.0 fusion.66
  507.0 36.9 %pmax.7 = f32[16]{0:T(128)S(1)} all-reduce(f32[16]{0:T(128)S(1)} %get-tuple-element.41), channel_id=1, replica_groups=mesh['grp'=2,'ep'=16] {'grp','ep'}, use_global_device_ids=true, to_apply=%region_19.21 | all-reduce | flops 16 | bytes 128 | tf_op jit(solution)/shard_map/pmax | solution.py:151
  545.4 41.4 %psum.15 = f32[16]{0:T(128)S(1)} all-reduce(f32[16]{0:T(128)S(1)} %exponential_reduce_fusion), channel_id=1, replica_groups=mesh['grp'=2,'ep'=16] {'grp','ep'}, use_global_device_ids=true, to_apply=%region_21.23 | all-reduce | flops 16 | bytes 128 | tf_op jit(solution)/shard_map/psum | solution.py:152
  (163 shorter events, 59.7 us)
Async XLA Ops:
  20.2 10.3 %copy-start.3 = (bf16[1,1024,512]{2,1,0:T(8,128)(2,1)S(1)}, bf16[1,1024,512]{2,1,0:T(8,128)(2,1)}, u32[]{:S(2)}) copy-start(bf16[1,1024,512]{2,1,0:T(8,128)(2,1)} %param.20) | copy-start | bytes 3145732
  22.9 30.6 %all-to-all-start.3 = ((bf16[16,2,16384]{2,1,0:T(2,128)(2,1)}), bf16[16,2,16384]{2,1,0:T(2,128)(2,1)}, u32[]{:S(2)}, u32[]{:S(2)}) async-start(bf16[16,2,16384]{2,1,0:T(2,128)(2,1)} %reshape.363), calls=%async_computation.3 | async-start | bytes 2097152 | tf_op jit(solution)/shard_map/all_to_all | solution.py:99
  40.9 20.3 %copy-start.15 = (s32[16]{0:T(128)S(1)}, s32[16]{0:T(128)}, u32[]{:S(2)}) copy-start(s32[16]{0:T(128)} %param.22) | copy-start | bytes 196
  40.9 20.4 %copy-start.14 = (s32[16]{0:T(128)S(1)}, s32[16]{0:T(128)}, u32[]{:S(2)}) copy-start(s32[16]{0:T(128)} %param.23) | copy-start | bytes 196
  40.9 20.5 %copy-start.10 = (s32[2,40,8]{1,2,0:T(8,128)S(1)}, s32[2,40,8]{1,2,0:T(8,128)}, u32[]{:S(2)}) copy-start(s32[2,40,8]{1,2,0:T(8,128)} %param.15) | copy-start | bytes 7684
  40.9 20.8 %copy-start.2 = (bf16[1,256,2048]{2,1,0:T(8,128)(2,1)S(1)}, bf16[1,256,2048]{2,1,0:T(8,128)(2,1)}, u32[]{:S(2)}) copy-start(bf16[1,256,2048]{2,1,0:T(8,128)(2,1)} %param.21) | copy-start | bytes 3145732
  53.5 29.9 %all-to-all-start.5 = ((bf16[16,2,16384]{2,1,0:T(2,128)(2,1)}), bf16[16,2,16384]{2,1,0:T(2,128)(2,1)}, u32[]{:S(2)}, u32[]{:S(2)}) async-start(bf16[16,2,16384]{2,1,0:T(2,128)(2,1)} %reshape.359), calls=%async_computation.5 | async-start | bytes 2097152 | tf_op jit(solution)/shard_map/all_to_all | solution.py:100
  60.4 240.1 %all-gather.7.cloned.1.call-start = ((), (), s32[]{:S(2)}) async-start(), calls=%async_computation.10 | async-start | bytes 3145728 | tf_op jit(solution)/shard_map/all_gather | solution.py:51
  74.0 18.1 %copy-start.6 = (bf16[2,40,2048]{2,1,0:T(8,128)(2,1)S(1)}, bf16[2,40,2048]{2,1,0:T(8,128)(2,1)}, u32[]{:S(2)}) copy-start(bf16[2,40,2048]{2,1,0:T(8,128)(2,1)} %param.14) | copy-start | bytes 983044
  74.0 18.3 %copy-start.12 = (f32[2048]{0:T(1024)S(1)}, f32[2048]{0:T(1024)}, u32[]{:S(2)}) copy-start(f32[2048]{0:T(1024)} %param.17) | copy-start | bytes 24580
  83.4 30.2 %all-to-all-start.7 = ((bf16[16,2,16384]{2,1,0:T(2,128)(2,1)}), bf16[16,2,16384]{2,1,0:T(2,128)(2,1)S(1)}, u32[]{:S(2)}, u32[]{:S(2)}) async-start(bf16[16,2,16384]{2,1,0:T(2,128)(2,1)} %reshape.355), calls=%async_computation.7 | async-start | bytes 2097152 | tf_op jit(solution)/shard_map/all_to_all | solution.py:101
  113.6 1.0 copy-start.4
  114.6 48.1 %all-to-all-start.2 = ((bf16[16,30,2048]{2,1,0:T(8,128)(2,1)}), bf16[16,30,2048]{2,1,0:T(8,128)(2,1)}, u32[]{:S(2)}, u32[]{:S(2)}) async-start(bf16[16,30,2048]{2,1,0:T(8,128)(2,1)} %reshape.264), calls=%async_computation.2 | async-start | bytes 4194304 | tf_op jit(solution)/shard_map/all_to_all | solution.py:127
  121.5 182.7 %all-gather.11.cloned.1.call-start = ((), (), s32[]{:S(2)}) async-start(), calls=%async_computation.12 | async-start | bytes 3145728 | tf_op jit(solution)/shard_map/all_gather | solution.py:63
  162.7 52.4 %all-to-all-start = ((bf16[16,30,2048]{2,1,0:T(8,128)(2,1)}), bf16[16,30,2048]{2,1,0:T(8,128)(2,1)}, u32[]{:S(2)}, u32[]{:S(2)}) async-start(bf16[16,30,2048]{2,1,0:T(8,128)(2,1)} %reshape.258), calls=%async_computation | async-start | bytes 4194304 | tf_op jit(solution)/shard_map/all_to_all | solution.py:127
  215.1 34.2 %all-to-all-start.4 = ((bf16[16,1,1024,32]{2,3,1,0:T(8,128)(2,1)}), bf16[16,1,1024,32]{2,3,1,0:T(8,128)(2,1)S(1)}, u32[]{:S(2)}, u32[]{:S(2)}) async-start(bf16[16,1,1024,32]{2,3,1,0:T(8,128)(2,1)} %fusion.38), calls=%async_computation.4 | async-start | bytes 2097152 | tf_op jit(solution)/shard_map/all_to_all | solution.py:108
  226.3 77.9 %all-gather.9.cloned.1.call-start = ((), (), s32[]{:S(2)}) async-start(), calls=%async_computation.11 | async-start | bytes 3145728 | tf_op jit(solution)/shard_map/all_gather | solution.py:56
  240.3 16.5 %copy-start.5 = (bf16[16,2,16384]{2,1,0:T(2,128)(2,1)S(1)}, bf16[16,2,16384]{2,1,0:T(2,128)(2,1)}, u32[]{:S(2)}) copy-start(bf16[16,2,16384]{2,1,0:T(2,128)(2,1)} %copy-done.4) | copy-start | bytes 3145732
  249.3 7.1 %copy-start = (bf16[16,1,1024,32]{2,3,1,0:T(8,128)(2,1)}, bf16[16,1,1024,32]{2,3,1,0:T(8,128)(2,1)S(1)}, u32[]{:S(2)}) copy-start(bf16[16,1,1024,32]{2,3,1,0:T(8,128)(2,1)S(1)} %all-to-all-done.4) | copy-start | bytes 3145732
  249.3 34.8 %all-to-all-start.6 = ((bf16[16,2,16384]{2,1,0:T(2,128)(2,1)}), bf16[16,2,16384]{2,1,0:T(2,128)(2,1)}, u32[]{:S(2)}, u32[]{:S(2)}) async-start(bf16[16,2,16384]{2,1,0:T(2,128)(2,1)} %reshape.361), calls=%async_computation.6 | async-start | bytes 2097152 | tf_op jit(solution)/shard_map/all_to_all | solution.py:113
  256.2 70.9 %all-gather.13.cloned.1.call-start = ((), (), s32[]{:S(2)}) async-start(), calls=%async_computation.13 | async-start | bytes 3145728 | tf_op jit(solution)/shard_map/all_gather | solution.py:51
  284.1 29.3 %all-to-all-start.8 = ((bf16[16,2,16384]{2,1,0:T(2,128)(2,1)}), bf16[16,2,16384]{2,1,0:T(2,128)(2,1)S(1)}, u32[]{:S(2)}, u32[]{:S(2)}) async-start(bf16[16,2,16384]{2,1,0:T(2,128)(2,1)} %reshape.357), calls=%async_computation.8 | async-start | bytes 2097152 | tf_op jit(solution)/shard_map/all_to_all | solution.py:114
  290.0 43.2 %all-gather.15.cloned.1.call-start = ((), (), s32[]{:S(2)}) async-start(), calls=%async_computation.14 | async-start | bytes 3145728 | tf_op jit(solution)/shard_map/all_gather | solution.py:56
  313.4 63.7 %all-to-all-start.1 = ((bf16[16,30,2048]{2,1,0:T(8,128)(2,1)}), bf16[16,30,2048]{2,1,0:T(8,128)(2,1)}, u32[]{:S(2)}, u32[]{:S(2)}) async-start(bf16[16,30,2048]{2,1,0:T(8,128)(2,1)} %reshape.260), calls=%async_computation.1 | async-start | bytes 4194304 | tf_op jit(solution)/shard_map/all_to_all | solution.py:129
  319.9 48.5 %all-gather.17.cloned.1.call-start = ((), (), s32[]{:S(2)}) async-start(), calls=%async_computation.15 | async-start | bytes 3145728 | tf_op jit(solution)/shard_map/all_gather | solution.py:63
  377.0 7.2 %copy-start.11 = (f32[2,40,8]{1,2,0:T(8,128)S(1)}, f32[2,40,8]{1,2,0:T(8,128)}, u32[]{:S(2)}) copy-start(f32[2,40,8]{1,2,0:T(8,128)} %param.16) | copy-start | bytes 7684
  377.1 7.7 %copy-start.13 = (s32[2,1,4]{2,1,0:T(1,128)S(1)}, s32[2,1,4]{2,1,0:T(1,128)}, u32[]{:S(2)}) copy-start(s32[2,1,4]{2,1,0:T(1,128)} %param.24) | copy-start | bytes 100
  377.1 47.1 %all-to-all-start.9 = ((bf16[16,30,2048]{2,1,0:T(8,128)(2,1)}), bf16[16,30,2048]{2,1,0:T(8,128)(2,1)}, u32[]{:S(2)}, u32[]{:S(2)}) async-start(bf16[16,30,2048]{2,1,0:T(8,128)(2,1)} %reshape.273), calls=%async_computation.9 | async-start | bytes 4194304 | tf_op jit(solution)/shard_map/all_to_all | solution.py:129
  428.4 1.3 copy-start.7
  428.4 74.6 %copy-start.9 = (f32[2048]{0:T(1024)S(1)}, f32[2048]{0:T(1024)}, u32[]{:S(2)}) copy-start(f32[2048]{0:T(1024)} %param.18) | copy-start | bytes 24580
  430.8 76.2 %copy-start.8 = (bf16[2,40,2048]{2,1,0:T(8,128)(2,1)}, bf16[2,40,2048]{2,1,0:T(8,128)(2,1)S(1)}, u32[]{:S(2)}) copy-start(bf16[2,40,2048]{2,1,0:T(8,128)(2,1)S(1)} %pad_maximum_fusion) | copy-start | bytes 983044
  503.1 41.1 %copy-start.1 = (bf16[16,1,1024,32]{2,3,1,0:T(8,128)(2,1)S(1)}, bf16[16,1,1024,32]{2,3,1,0:T(8,128)(2,1)}, u32[]{:S(2)}) copy-start(bf16[16,1,1024,32]{2,3,1,0:T(8,128)(2,1)} %copy-done) | copy-start | bytes 3145732
Sparse Core Ops, SparseCore 0:
  62.8 34.3 all-gather.6
  123.9 34.3 all-gather.10
  228.7 34.4 all-gather.8
  264.6 33.1 all-gather.12
  299.7 33.5 all-gather.14
  335.2 33.1 all-gather.16
